TPU v7x, 32 devices: a whole 2x2x4 slice. The times are simulated.
32 devices in a mesh: groups: 2 (over x), rows: 16 (over z, y, core).
Axes of the slice: x: 2, y: 2, z: 4, core: 2. Of those that a mesh axis runs over, the one named last changes fastest.
Arguments:
- source: float32 [64, 4096], P(None, ('groups', 'rows')), parts along dimension 1, may hold values from -48 to 48
- target: float32 [64, 4096], P(None, ('groups', 'rows')), parts along dimension 1, may hold values from -48 to 48
Outputs:
- source_potential: float32 [4096], P(('groups', 'rows')), parts along dimension 0
- target_potential: float32 [4096], P(('groups', 'rows')), parts along dimension 0
- grad_source: float32 [64, 4096], P(None, ('groups', 'rows')), parts along dimension 1
- grad_target: float32 [64, 4096], P(None, ('groups', 'rows')), parts along dimension 1
There are 2 independent parts, one for each index of `groups`. A program takes and returns all parts, laid end to end along the dimension named above; each array names one. Nothing has to cross between parts.
All inputs are finite; a program needn't handle non-finite values.
Results may differ from a plain program's by a relative error of at most 0.0003.
Values sent between devices are 32-bit elements; how exact they have to be, the bound alone decides.
A program may use at most 64 MiB of HBM per device.

v0:
```python
import math
import jax
import jax.numpy as jnp
from jax import lax
from jax.sharding import PartitionSpec as P

ITERS = 4
softness = 0.2
block_width = 512


def tile_scores(left, left_sq, right, potential):
    cross = lax.dot_general(
        left,
        right,
        (((0,), (0,)), ((), ())),
        precision=lax.Precision.HIGHEST,
        preferred_element_type=jnp.float32,
    )
    right_sq = jnp.sum(right * right, axis=0)
    cost = (left_sq[:, None] + right_sq[None, :] - 2.0 * cross) / left.shape[0]
    return (potential[None, :] - cost) / softness


def absorb(running, left, left_sq, right, potential):
    scores = tile_scores(left, left_sq, right, potential)
    maxima = running[0]
    new_max = jnp.maximum(maxima, jnp.max(scores, axis=1))
    shrink = jnp.exp(maxima - new_max)
    weights = jnp.exp(scores - new_max[:, None])
    totals = running[1] * shrink + jnp.sum(weights, axis=1)
    if len(running) == 3:
        weighted = running[2] * shrink[None, :] + lax.dot_general(
            right,
            weights,
            (((1,), (1,)), ((), ())),
            precision=lax.Precision.HIGHEST,
            preferred_element_type=jnp.float32,
        )
        return (new_max, totals, weighted)
    return (new_max, totals)


def make_folder(left):
    left_sq = jnp.sum(left * left, axis=0)

    def folder(running, pieces, offset):
        right = pieces[0]
        potential = pieces[1][0]
        columns = right.shape[1]
        blocks = columns // block_width
        right_blocks = jnp.moveaxis(right.reshape(right.shape[0], blocks, block_width), 1, 0)
        pot_blocks = potential.reshape(blocks, block_width)

        def advance(inner, member):
            return (absorb(inner, left, left_sq, member[0], member[1]), None)

        running, unused = lax.scan(advance, running, (right_blocks, pot_blocks))
        return running

    return folder


def potential_of(maxima, totals, log_count):
    return -softness * (log_count + maxima + jnp.log(totals))


def column_partial(right, source, f_block):
    right_sq = jnp.sum(right * right, axis=0)
    scores = tile_scores(right, right_sq, source, f_block)
    maxima = jnp.max(scores, axis=1)
    totals = jnp.sum(jnp.exp(scores - maxima[:, None]), axis=1)
    return (maxima, totals)


def replicated_columns(source, target, f_block, log_count):
    local_count = source.shape[1]
    pieces = lax.all_gather(target, "rows", axis=1, tiled=True)
    columns = pieces.shape[1]
    blocks = columns // block_width
    right_blocks = jnp.moveaxis(pieces.reshape(pieces.shape[0], blocks, block_width), 1, 0)
    stats = lax.map(lambda member: column_partial(member, source, f_block), right_blocks)
    maxima = stats[0].reshape(columns)
    totals = stats[1].reshape(columns)
    maxima, totals = (maxima, totals)
    global_max = lax.pmax(maxima, "rows")
    summed = lax.psum(totals * jnp.exp(maxima - global_max), "rows")
    log_total = global_max + jnp.log(summed)
    g_all = -softness * (log_count + log_total)
    return lax.dynamic_slice_in_dim(g_all, lax.axis_index("rows") * local_count, local_count, 0)


def local(source, target):
    features, local_count = source.shape
    log_count = math.log(local_count * lax.axis_size("rows"))
    source_folder = make_folder(source)
    target_folder = make_folder(target)
    initial = (jnp.full((local_count,), -1e30, jnp.float32), jnp.zeros((local_count,), jnp.float32))
    with_mean = initial + (jnp.zeros((features, local_count), jnp.float32),)
    g_block = jnp.zeros((local_count,), jnp.float32)
    f_block = jnp.zeros((local_count,), jnp.float32)
    for step_index in range(ITERS):
        maxima, totals = source_folder(
            initial,
            (
                lax.all_gather(target, "rows", axis=1, tiled=True),
                lax.all_gather(g_block[None, :], "rows", axis=1, tiled=True),
            ),
            jnp.int32(0),
        )
        f_block = potential_of(maxima, totals, log_count)
        g_block = replicated_columns(source, target, f_block, log_count)
    maxima, totals, weighted = source_folder(
        with_mean,
        (
            lax.all_gather(target, "rows", axis=1, tiled=True),
            lax.all_gather(g_block[None, :], "rows", axis=1, tiled=True),
        ),
        jnp.int32(0),
    )
    row_mass = jnp.exp(f_block / softness + maxima + jnp.log(totals) + log_count)
    grad_source = row_mass[None, :] * (source - weighted / totals[None, :])
    col_max, col_totals, col_weighted = target_folder(
        with_mean,
        (
            lax.all_gather(source, "rows", axis=1, tiled=True),
            lax.all_gather(f_block[None, :], "rows", axis=1, tiled=True),
        ),
        jnp.int32(0),
    )
    grad_target = target - col_weighted / col_totals[None, :]
    return (f_block, g_block, grad_source, grad_target)


def solution(mesh):
    return jax.shard_map(
        local,
        mesh=mesh,
        in_specs=(P(None, ("groups", "rows")), P(None, ("groups", "rows"))),
        out_specs=(
            P(("groups", "rows")),
            P(("groups", "rows")),
            P(None, ("groups", "rows")),
            P(None, ("groups", "rows")),
        ),
        check_vma=False,
    )
```

profile of v0, /device:TPU:0, one launch (start us, length us, event | category | flops | bytes accessed | tf_op | source)
XLA Modules:
  0.0 419.5 jit_solution(10222245431904502799)
XLA Ops:
  0.7 0.8 multiply_reduce_fusion.2
  1.5 24.6 %all_gather.14 = f32[64,2048]{1,0:T(8,128)S(1)} all-gather(f32[64,128]{1,0:T(8,128)S(1)} %copy-done.1), channel_id=1, replica_groups=mesh['groups'=2,'rows'=16] {'rows'}, dimensions={1}, use_global_device_ids=true | all-gather | bytes 557056 | tf_op jit(solution)/shard_map/all_gather | solution.py:106
  27.2 3.2 while.143
  30.4 2.8 while.139
  33.2 30.3 %pmax.28 = f32[2048]{0:T(1024)S(1)} all-reduce(f32[2048]{0:T(1024)S(1)} %bitcast.291), channel_id=1, replica_groups=mesh['groups'=2,'rows'=16] {'rows'}, use_global_device_ids=true, to_apply=%region_11.12 | all-reduce | flops 2048 | bytes 16384 | tf_op jit(solution)/shard_map/pmax | solution.py:86
  63.6 30.0 %psum.28 = f32[2048]{0:T(1024)S(1)} all-reduce(f32[2048]{0:T(1024)S(1)} %exponential_multiply_fusion.3), channel_id=1, replica_groups=mesh['groups'=2,'rows'=16] {'rows'}, use_global_device_ids=true, to_apply=%region_12.13 | all-reduce | flops 2048 | bytes 16384 | tf_op jit(solution)/shard_map/psum | solution.py:87
  93.7 17.0 %all-gather.5 = f32[16,1,128]{2,1,0:T(1,128)S(1)} all-gather(f32[1,1,128]{2,1,0:T(1,128)S(1)} %multiply_bitcast_fusion.2), channel_id=2, replica_groups=mesh['groups'=2,'rows'=16] {'rows'}, dimensions={0}, use_global_device_ids=true | all-gather | bytes 8704 | tf_op jit(solution)/shard_map/all_gather | solution.py:107
  111.8 3.4 while.144
  111.8 0.6 fusion.195
  112.7 0.6 fusion.195
  113.5 0.6 fusion.195
  114.4 0.6 fusion.195
  115.2 2.8 while.140
  118.0 31.9 %pmax.29 = f32[2048]{0:T(1024)S(1)} all-reduce(f32[2048]{0:T(1024)S(1)} %bitcast.293), channel_id=1, replica_groups=mesh['groups'=2,'rows'=16] {'rows'}, use_global_device_ids=true, to_apply=%region_23.24 | all-reduce | flops 2048 | bytes 16384 | tf_op jit(solution)/shard_map/pmax | solution.py:86
  149.9 30.0 %psum.29 = f32[2048]{0:T(1024)S(1)} all-reduce(f32[2048]{0:T(1024)S(1)} %exponential_multiply_fusion.2), channel_id=1, replica_groups=mesh['groups'=2,'rows'=16] {'rows'}, use_global_device_ids=true, to_apply=%region_24.25 | all-reduce | flops 2048 | bytes 16384 | tf_op jit(solution)/shard_map/psum | solution.py:87
  180.0 17.0 %all-gather.6 = f32[16,1,128]{2,1,0:T(1,128)S(1)} all-gather(f32[1,1,128]{2,1,0:T(1,128)S(1)} %multiply_bitcast_fusion.1), channel_id=3, replica_groups=mesh['groups'=2,'rows'=16] {'rows'}, dimensions={0}, use_global_device_ids=true | all-gather | bytes 8704 | tf_op jit(solution)/shard_map/all_gather | solution.py:107
  197.6 3.4 while.145
  197.7 0.6 fusion.200
  198.5 0.6 fusion.200
  199.3 0.6 fusion.200
  200.2 0.6 fusion.200
  201.0 2.8 while.141
  203.8 31.9 %pmax.30 = f32[2048]{0:T(1024)S(1)} all-reduce(f32[2048]{0:T(1024)S(1)} %bitcast.295), channel_id=1, replica_groups=mesh['groups'=2,'rows'=16] {'rows'}, use_global_device_ids=true, to_apply=%region_35.36 | all-reduce | flops 2048 | bytes 16384 | tf_op jit(solution)/shard_map/pmax | solution.py:86
  235.7 30.0 %psum.30 = f32[2048]{0:T(1024)S(1)} all-reduce(f32[2048]{0:T(1024)S(1)} %exponential_multiply_fusion.1), channel_id=1, replica_groups=mesh['groups'=2,'rows'=16] {'rows'}, use_global_device_ids=true, to_apply=%region_36.37 | all-reduce | flops 2048 | bytes 16384 | tf_op jit(solution)/shard_map/psum | solution.py:87
  265.8 17.0 %all-gather.7 = f32[16,1,128]{2,1,0:T(1,128)S(1)} all-gather(f32[1,1,128]{2,1,0:T(1,128)S(1)} %multiply_bitcast_fusion), channel_id=4, replica_groups=mesh['groups'=2,'rows'=16] {'rows'}, dimensions={0}, use_global_device_ids=true | all-gather | bytes 8704 | tf_op jit(solution)/shard_map/all_gather | solution.py:107
  283.4 3.4 while.146
  283.5 0.6 fusion.205
  284.3 0.6 fusion.205
  285.1 0.6 fusion.205
  286.0 0.6 fusion.205
  286.8 2.8 while.142
  289.6 31.9 %pmax.31 = f32[2048]{0:T(1024)S(1)} all-reduce(f32[2048]{0:T(1024)S(1)} %bitcast.297), channel_id=1, replica_groups=mesh['groups'=2,'rows'=16] {'rows'}, use_global_device_ids=true, to_apply=%region_47.48 | all-reduce | flops 2048 | bytes 16384 | tf_op jit(solution)/shard_map/pmax | solution.py:86
  321.5 30.0 %psum.31 = f32[2048]{0:T(1024)S(1)} all-reduce(f32[2048]{0:T(1024)S(1)} %exponential_multiply_fusion), channel_id=1, replica_groups=mesh['groups'=2,'rows'=16] {'rows'}, use_global_device_ids=true, to_apply=%region_48.49 | all-reduce | flops 2048 | bytes 16384 | tf_op jit(solution)/shard_map/psum | solution.py:87
  352.1 17.0 %all-gather.8 = f32[16,1,128]{2,1,0:T(1,128)S(1)} all-gather(f32[1,1,128]{2,1,0:T(1,128)S(1)} %bitcast.316), channel_id=5, replica_groups=mesh['groups'=2,'rows'=16] {'rows'}, dimensions={0}, use_global_device_ids=true | all-gather | bytes 8704 | tf_op jit(solution)/shard_map/all_gather | solution.py:117
  369.7 4.6 %while.147 = (s32[]{:T(128)}, f32[128]{0:T(128)S(1)}, f32[128]{0:T(128)S(1)}, f32[64,128]{1,0:T(8,128)S(1)}, f32[4,512]{1,0:T(4,128)S(1)}, /*index=5*/f32[128]{0...) while((s32[]{:T(128)}, f32[128]{0:T(128)S(1)}, ...), condition=%wide.region_53.54_spmd.clone, body=%wide.region_49.53_spmd.clone.sunk | while | flops 101408896 | bytes 1297033 | solution.py:58
  369.8 0.6 fusion.211
  371.0 0.6 fusion.211
  372.1 0.6 fusion.211
  373.3 0.6 fusion.211
  374.4 0.6 subtract_multiply_fusion
  375.1 19.0 %all-gather.9 = f32[16,1,128]{2,1,0:T(1,128)S(1)} all-gather(f32[1,1,128]{2,1,0:T(1,128)S(1)} %bitcast.317), channel_id=6, replica_groups=mesh['groups'=2,'rows'=16] {'rows'}, dimensions={0}, use_global_device_ids=true | all-gather | bytes 8704 | tf_op jit(solution)/shard_map/all_gather | solution.py:127
  394.6 18.8 %all_gather.36 = f32[64,2048]{1,0:T(8,128)S(1)} all-gather(f32[64,128]{1,0:T(8,128)S(1)} %get-tuple-element.1822), channel_id=1, replica_groups=mesh['groups'=2,'rows'=16] {'rows'}, dimensions={1}, use_global_device_ids=true | all-gather | bytes 557056 | tf_op jit(solution)/shard_map/all_gather | solution.py:126
  413.8 5.1 %while.148 = (s32[]{:T(128)}, f32[128]{0:T(128)S(1)}, f32[128]{0:T(128)S(1)}, f32[64,128]{1,0:T(8,128)S(1)}, f32[4,512]{1,0:T(4,128)S(1)}, /*index=5*/f32[128]{0...) while((s32[]{:T(128)}, f32[128]{0:T(128)S(1)}, ...), condition=%wide.region_59.60_spmd.clone, body=%wide.region_55.59_spmd.clone.sunk | while | flops 101408896 | bytes 1559169 | solution.py:58
  414.0 0.6 fusion.216
  415.3 0.6 fusion.216
  416.5 0.6 fusion.216
  417.8 0.6 fusion.216
  418.9 0.6 divide_subtract_fusion
  (302 shorter events, 25.7 us)
Async XLA Ops:
  0.6 0.9 copy-start.1
  26.4 0.8 copy-start
  289.6 85.5 %copy-start.3 = (f32[128]{0:T(128)}, f32[128]{0:T(128)S(1)}, u32[]{:S(2)}) copy-start(f32[128]{0:T(128)S(1)} %get-tuple-element.1832) | copy-start | bytes 1540
  351.6 0.5 copy-start.2
where the time goes:
time: 420 us
  blocking collectives  376 us (90%)
  matrix products  25.4 us (6%)
  other arithmetic  10.4 us (2%)
  local copies, waits for them, and re-layouts  4.82 us (1%)
    pmax x4, blocking collectives, replicated_columns(): global_max = lax.pmax(maxima, 'rows')  126 us
    psum x4, blocking collectives, replicated_columns(): summed = lax.psum(totals * jnp.exp(maxima - global_max), 'rows')  120 us
    all_gather x4, blocking collectives, local(): lax.all_gather(g_block[None, :], 'rows', axis=1, tiled=True)  68.1 us
    all_gather x1, blocking collectives, local(): lax.all_gather(target, 'rows', axis=1, tiled=True)  24.6 us
    dot_general x40, matrix products, tile_scores(): lax.dot_general(left, right, (((0,), (0,)), ((), ())), precision=lax.Prec...  22.9 us
    all_gather x1, blocking collectives, local(): lax.all_gather(f_block[None, :], 'rows', axis=1, tiled=True)  19 us
    all_gather x1, blocking collectives, local(): lax.all_gather(source, 'rows', axis=1, tiled=True)  18.8 us

commit v1 on v0

--- a/solution.py
+++ b/solution.py
@@ -84,7 +84,7 @@
     totals = stats[1].reshape(columns)
     maxima, totals = (maxima, totals)
     global_max = lax.pmax(maxima, "rows")
-    summed = lax.psum(totals * jnp.exp(maxima - global_max), "rows")
+    summed = jnp.sum(lax.all_gather(totals * jnp.exp(maxima - global_max), "rows"), axis=0)
     log_total = global_max + jnp.log(summed)
     g_all = -softness * (log_count + log_total)
     return lax.dynamic_slice_in_dim(g_all, lax.axis_index("rows") * local_count, local_count, 0)

time: 420 us -> 373 us (0.89)
  blocking collectives: 376 us -> 329 us
    psum x4 -> x0, blocking collectives: 120 us -> none  [replicated_columns(): summed = lax.psum(totals * jnp.exp(maxima - global_max), 'rows')]
    all_gather x0 -> x4, blocking collectives: none -> 69.9 us  [replicated_columns(): lax.all_gather(totals * jnp.exp(maxima - global_max), 'rows')]
    all_gather x4, blocking collectives: 68.1 us -> 75.8 us  [local(): lax.all_gather(g_block[None, :], 'rows', axis=1, tiled=True)]
    pmax x4, blocking collectives: 126 us -> 121 us  [replicated_columns(): global_max = lax.pmax(maxima, 'rows')]
where the time goes in v1:
time: 373 us
  blocking collectives  329 us (88%)
  matrix products  25.4 us (7%)
  other arithmetic  10.5 us (3%)
  local copies, waits for them, and re-layouts  4.93 us (1%)
    pmax x4, blocking collectives, replicated_columns(): global_max = lax.pmax(maxima, 'rows')  121 us
    all_gather x4, blocking collectives, local(): lax.all_gather(g_block[None, :], 'rows', axis=1, tiled=True)  75.8 us
    all_gather x4, blocking collectives, replicated_columns(): lax.all_gather(totals * jnp.exp(maxima - global_max), 'rows')  69.9 us
    all_gather x1, blocking collectives, local(): lax.all_gather(target, 'rows', axis=1, tiled=True)  24.6 us
    dot_general x40, matrix products, tile_scores(): lax.dot_general(left, right, (((0,), (0,)), ((), ())), precision=lax.Prec...  22.9 us
    all_gather x1, blocking collectives, local(): lax.all_gather(source, 'rows', axis=1, tiled=True)  20.4 us
    all_gather x1, blocking collectives, local(): lax.all_gather(f_block[None, :], 'rows', axis=1, tiled=True)  17.3 us

profile of v1, /device:TPU:0, one launch (start us, length us, event | category | flops | bytes accessed | tf_op | source)
XLA Modules:
  0.0 372.6 jit_solution(9475247896817435845)
XLA Ops:
  0.7 0.8 multiply_reduce_fusion.2
  1.5 24.6 %all_gather.54 = f32[64,2048]{1,0:T(8,128)S(1)} all-gather(f32[64,128]{1,0:T(8,128)S(1)} %copy-done.1), channel_id=1, replica_groups=mesh['groups'=2,'rows'=16] {'rows'}, dimensions={1}, use_global_device_ids=true | all-gather | bytes 557056 | tf_op jit(solution)/shard_map/all_gather | solution.py:106
  27.2 3.2 while.143
  30.4 2.8 while.139
  33.2 30.3 %pmax.28 = f32[2048]{0:T(1024)S(1)} all-reduce(f32[2048]{0:T(1024)S(1)} %bitcast.291), channel_id=1, replica_groups=mesh['groups'=2,'rows'=16] {'rows'}, use_global_device_ids=true, to_apply=%region_11.12 | all-reduce | flops 2048 | bytes 16384 | tf_op jit(solution)/shard_map/pmax | solution.py:86
  63.6 17.5 %all-gather = f32[32768]{0:T(1024)S(1)} all-gather(f32[2048]{0:T(1024)S(1)} %exponential_multiply_fusion.3), channel_id=2, replica_groups=mesh['groups'=2,'rows'=16] {'rows'}, dimensions={0}, use_global_device_ids=true | all-gather | bytes 139264 | tf_op jit(solution)/shard_map/all_gather | solution.py:87
  81.2 19.0 %all-gather.9 = f32[16,1,128]{2,1,0:T(1,128)S(1)} all-gather(f32[1,1,128]{2,1,0:T(1,128)S(1)} %multiply_bitcast_fusion.2), channel_id=3, replica_groups=mesh['groups'=2,'rows'=16] {'rows'}, dimensions={0}, use_global_device_ids=true | all-gather | bytes 8704 | tf_op jit(solution)/shard_map/all_gather | solution.py:107
  101.3 3.4 while.144
  101.3 0.6 fusion.195
  102.2 0.6 fusion.195
  103.0 0.6 fusion.195
  103.9 0.6 fusion.195
  104.7 2.8 while.140
  107.5 30.3 %pmax.29 = f32[2048]{0:T(1024)S(1)} all-reduce(f32[2048]{0:T(1024)S(1)} %bitcast.293), channel_id=1, replica_groups=mesh['groups'=2,'rows'=16] {'rows'}, use_global_device_ids=true, to_apply=%region_23.24 | all-reduce | flops 2048 | bytes 16384 | tf_op jit(solution)/shard_map/pmax | solution.py:86
  137.8 17.5 %all-gather.2 = f32[32768]{0:T(1024)S(1)} all-gather(f32[2048]{0:T(1024)S(1)} %exponential_multiply_fusion.2), channel_id=4, replica_groups=mesh['groups'=2,'rows'=16] {'rows'}, dimensions={0}, use_global_device_ids=true | all-gather | bytes 139264 | tf_op jit(solution)/shard_map/all_gather | solution.py:87
  155.4 19.0 %all-gather.10 = f32[16,1,128]{2,1,0:T(1,128)S(1)} all-gather(f32[1,1,128]{2,1,0:T(1,128)S(1)} %multiply_bitcast_fusion.1), channel_id=5, replica_groups=mesh['groups'=2,'rows'=16] {'rows'}, dimensions={0}, use_global_device_ids=true | all-gather | bytes 8704 | tf_op jit(solution)/shard_map/all_gather | solution.py:107
  175.0 3.4 while.145
  175.0 0.6 fusion.200
  175.9 0.6 fusion.200
  176.7 0.6 fusion.200
  177.6 0.6 fusion.200
  178.4 2.8 while.141
  181.2 30.3 %pmax.30 = f32[2048]{0:T(1024)S(1)} all-reduce(f32[2048]{0:T(1024)S(1)} %bitcast.295), channel_id=1, replica_groups=mesh['groups'=2,'rows'=16] {'rows'}, use_global_device_ids=true, to_apply=%region_35.36 | all-reduce | flops 2048 | bytes 16384 | tf_op jit(solution)/shard_map/pmax | solution.py:86
  211.5 17.5 %all-gather.4 = f32[32768]{0:T(1024)S(1)} all-gather(f32[2048]{0:T(1024)S(1)} %exponential_multiply_fusion.1), channel_id=6, replica_groups=mesh['groups'=2,'rows'=16] {'rows'}, dimensions={0}, use_global_device_ids=true | all-gather | bytes 139264 | tf_op jit(solution)/shard_map/all_gather | solution.py:87
  229.1 19.0 %all-gather.11 = f32[16,1,128]{2,1,0:T(1,128)S(1)} all-gather(f32[1,1,128]{2,1,0:T(1,128)S(1)} %multiply_bitcast_fusion), channel_id=7, replica_groups=mesh['groups'=2,'rows'=16] {'rows'}, dimensions={0}, use_global_device_ids=true | all-gather | bytes 8704 | tf_op jit(solution)/shard_map/all_gather | solution.py:107
  248.7 3.4 while.146
  248.8 0.6 fusion.205
  249.6 0.6 fusion.205
  250.4 0.6 fusion.205
  251.3 0.6 fusion.205
  252.1 2.8 while.142
  254.9 30.3 %pmax.31 = f32[2048]{0:T(1024)S(1)} all-reduce(f32[2048]{0:T(1024)S(1)} %bitcast.297), channel_id=1, replica_groups=mesh['groups'=2,'rows'=16] {'rows'}, use_global_device_ids=true, to_apply=%region_47.48 | all-reduce | flops 2048 | bytes 16384 | tf_op jit(solution)/shard_map/pmax | solution.py:86
  285.2 17.5 %all-gather.6 = f32[32768]{0:T(1024)S(1)} all-gather(f32[2048]{0:T(1024)S(1)} %exponential_multiply_fusion), channel_id=8, replica_groups=mesh['groups'=2,'rows'=16] {'rows'}, dimensions={0}, use_global_device_ids=true | all-gather | bytes 139264 | tf_op jit(solution)/shard_map/all_gather | solution.py:87
  303.4 19.0 %all-gather.12 = f32[16,1,128]{2,1,0:T(1,128)S(1)} all-gather(f32[1,1,128]{2,1,0:T(1,128)S(1)} %bitcast.316), channel_id=9, replica_groups=mesh['groups'=2,'rows'=16] {'rows'}, dimensions={0}, use_global_device_ids=true | all-gather | bytes 8704 | tf_op jit(solution)/shard_map/all_gather | solution.py:117
  322.9 4.6 %while.147 = (s32[]{:T(128)}, f32[128]{0:T(128)S(1)}, f32[128]{0:T(128)S(1)}, f32[64,128]{1,0:T(8,128)S(1)}, f32[4,512]{1,0:T(4,128)S(1)}, /*index=5*/f32[128]{0...) while((s32[]{:T(128)}, f32[128]{0:T(128)S(1)}, ...), condition=%wide.region_53.54_spmd.clone, body=%wide.region_49.53_spmd.clone.sunk | while | flops 101408896 | bytes 1297033 | solution.py:58
  323.0 0.6 fusion.211
  324.2 0.6 fusion.211
  325.3 0.6 fusion.211
  326.5 0.6 fusion.211
  327.6 0.6 subtract_multiply_fusion
  328.2 17.3 %all-gather.13 = f32[16,1,128]{2,1,0:T(1,128)S(1)} all-gather(f32[1,1,128]{2,1,0:T(1,128)S(1)} %bitcast.317), channel_id=10, replica_groups=mesh['groups'=2,'rows'=16] {'rows'}, dimensions={0}, use_global_device_ids=true | all-gather | bytes 8704 | tf_op jit(solution)/shard_map/all_gather | solution.py:127
  346.1 20.4 %all_gather.68 = f32[64,2048]{1,0:T(8,128)S(1)} all-gather(f32[64,128]{1,0:T(8,128)S(1)} %get-tuple-element.1893), channel_id=1, replica_groups=mesh['groups'=2,'rows'=16] {'rows'}, dimensions={1}, use_global_device_ids=true | all-gather | bytes 557056 | tf_op jit(solution)/shard_map/all_gather | solution.py:126
  366.8 5.1 %while.148 = (s32[]{:T(128)}, f32[128]{0:T(128)S(1)}, f32[128]{0:T(128)S(1)}, f32[64,128]{1,0:T(8,128)S(1)}, f32[4,512]{1,0:T(4,128)S(1)}, /*index=5*/f32[128]{0...) while((s32[]{:T(128)}, f32[128]{0:T(128)S(1)}, ...), condition=%wide.region_59.60_spmd.clone, body=%wide.region_55.59_spmd.clone.sunk | while | flops 101408896 | bytes 1559169 | solution.py:58
  367.0 0.6 fusion.216
  368.3 0.6 fusion.216
  369.6 0.6 fusion.216
  370.9 0.6 fusion.216
  371.9 0.6 divide_subtract_fusion
  (310 shorter events, 25.9 us)
Async XLA Ops:
  0.6 0.9 copy-start.1
  26.4 0.8 copy-start
  254.9 73.4 %copy-start.3 = (f32[128]{0:T(128)}, f32[128]{0:T(128)S(1)}, u32[]{:S(2)}) copy-start(f32[128]{0:T(128)S(1)} %get-tuple-element.1903) | copy-start | bytes 1540
  302.9 0.5 copy-start.2
